TPU v7x, 256 devices: a whole 4x4x8 slice. The times are simulated.
256 devices in a mesh: row: 16 (over x_lo, z), col: 16 (over x_hi, y, core).
Axes of the slice: x: 4 (x_hi: 2, x_lo: 2; x = x_hi * 2 + x_lo), y: 4, z: 8, core: 2. Of those that a mesh axis runs over, the one named last changes fastest.
Arguments:
- points: bfloat16 [96, 1024, 1024], P('row', 'col')
- targets: bfloat16 [96, 1024, 1000], P('row', 'col'), may hold values from -6 to 6
- coeffs: float32 [96, 1024, 1000], P('row', 'col'), may hold values from -0.25 to 0.25
- block_inverse: float32 [96, 1024, 1024], P('row', 'col')
- block_order: int32 [96], replicated, may hold values from 0 to 95, each once
Outputs:
- coeffs_out: float32 [96, 1024, 1000], P('row', 'col')
All inputs are finite; a program needn't handle non-finite values.
Results may differ from a plain program's by a relative error of at most 0.0003.
Values may be sent and summed in bfloat16 or wider, within the bound.
A program may use at most 64 MiB of HBM per device.

v0:
```python
import jax
import jax.numpy as jnp
from jax import lax
from jax.sharding import PartitionSpec as P

STEPS = 2
ridge_weight = 1.0


def broadcast(value, axis, source):
    kept = jnp.where(lax.axis_index(axis) == source, value, 0).astype(value.dtype)
    return lax.psum(kept, axis)


def on_device(points, targets, coeffs, block_inverse, block_order):
    blocks_here, per_col, features = points.shape
    classes = targets.shape[2]
    my_row = lax.axis_index("row")
    my_col = lax.axis_index("col")
    flat_points = points.reshape(blocks_here * per_col, features)
    flat_wide = flat_points.astype(jnp.float32)
    point_squares = jnp.sum(flat_wide * flat_wide, axis=1)
    current = coeffs
    for sweep_step in range(STEPS):
        block_id = block_order[sweep_step]
        local_index = block_id % blocks_here
        owner_row = block_id // blocks_here
        own_slice = lax.dynamic_index_in_dim(points, local_index, 0, keepdims=False)
        full_block = lax.all_gather(own_slice, "col", axis=0, tiled=True)
        active = broadcast(full_block, "row", owner_row)
        active_wide = active.astype(jnp.float32)
        active_squares = jnp.sum(active_wide * active_wide, axis=1)
        inner = lax.dot_general(
            active, flat_points, (((1,), (1,)), ((), ())), preferred_element_type=jnp.float32
        )
        distance = active_squares[:, None] + point_squares[None, :] - 2.0 * inner
        tile_wide = jnp.exp(-distance * (0.5 / features))
        flat_current = current.reshape(blocks_here * per_col, classes)
        products = jnp.dot(
            tile_wide,
            flat_current,
            precision=lax.Precision.HIGHEST,
            preferred_element_type=jnp.float32,
        )
        summed = lax.psum(products, ("row", "col"))
        own_sum = lax.dynamic_slice_in_dim(summed, my_col * per_col, per_col, 0)
        previous = lax.dynamic_index_in_dim(current, local_index, 0, keepdims=False)
        wanted = lax.dynamic_index_in_dim(targets, local_index, 0, keepdims=False).astype(
            jnp.float32
        )
        residual = wanted - own_sum - ridge_weight * previous
        full_residual = lax.all_gather(residual, "col", axis=0, tiled=True)
        inverse_rows = lax.dynamic_index_in_dim(block_inverse, local_index, 0, keepdims=False)
        increment = jnp.dot(
            inverse_rows,
            full_residual,
            precision=lax.Precision.HIGHEST,
            preferred_element_type=jnp.float32,
        )
        updated = jnp.where(my_row == owner_row, previous + increment, previous)
        current = lax.dynamic_update_index_in_dim(current, updated, local_index, 0)
    return current


def solution(mesh):
    placed = (
        P("row", "col", None),
        P("row", "col", None),
        P("row", "col", None),
        P("row", "col", None),
        P(),
    )
    return jax.shard_map(
        on_device, mesh=mesh, in_specs=placed, out_specs=P("row", "col", None), check_vma=False
    )
```

profile of v0, /device:TPU:1, one launch (start us, length us, event | category | flops | bytes accessed | tf_op | source)
XLA Modules:
  0.0 974.1 jit_solution(10416053570746938592)
XLA Ops:
  6.5 0.0 copy-start
  6.5 0.0 copy-start.5
  6.5 0.0 all-gather.13.cloned.1.call-start
  6.5 1.5 copy.13
  8.1 0.0 copy-done.5
  8.1 0.6 fusion.40
  9.8 1.7 constant_dynamic-slice_fusion.2
  11.5 0.0 all-gather.13.cloned.1.call-update
  11.5 0.0 all-gather.11.cloned.1.call-start
  11.6 0.7 all-gather.11.cloned.1.call-update
  12.3 0.0 all-reduce.9.cloned.1.call-start
  14.6 53.9 %all-gather.13.cloned.1.call-done = bf16[1,1024,1024]{2,1,0:T(8,128)(2,1)} async-done(((bf16[1,64,1024]{2,1,0:T(8,128)(2,1)}), bf16[1,1024,1024]{2,1,0:T(8,128)(2,1)}) %all-gather.13.cloned.1.call-update) | async-done | bytes 2097168 | tf_op jit(solution)/shard_map/all_gather | solution.py:29
  68.5 1.5 select_bitcast_fusion
  69.9 52.7 %all-gather.11.cloned.1.call-done = bf16[1,1024,1024]{2,1,0:T(8,128)(2,1)} async-done(((bf16[1,64,1024]{2,1,0:T(8,128)(2,1)}), bf16[1,1024,1024]{2,1,0:T(8,128)(2,1)}) %all-gather.11.cloned.1.call-update) | async-done | bytes 2097168 | tf_op jit(solution)/shard_map/all_gather | solution.py:29
  122.7 1.4 select_bitcast_fusion.1
  124.1 0.0 all-reduce.9.cloned.1.call-update
  124.1 0.0 all-reduce.5.cloned.1.call-start
  124.2 1.4 multiply_reduce_fusion.2
  125.6 0.1 add.75
  125.6 143.2 %all-reduce.9.cloned.1.call-done = (bf16[1024,1024]{1,0:T(8,128)(2,1)}, bf16[1024,1024]{1,0:T(8,128)(2,1)}) async-done(((bf16[1024,1024]{1,0:T(8,128)(2,1)}, bf16[1024,1024]{1,0:T(8,128)(2,1)}), (bf16[1024,1024]{1,0:T(8,128)(2,1)}, bf16[1024,1024]{1,0:T(8,128)(2,1)})) %all-reduce.9.cloned.1.call-update) | async-done | bytes 4194320 | tf_op jit(solution)/shard_map/psum | solution.py:12
  268.9 2.2 multiply_reduce_fusion.1
  271.1 0.0 copy-done.3
  271.1 2.4 fusion.41
  273.5 8.6 fusion.7
  282.1 0.0 all-reduce.5.cloned.1.call-update
  282.1 0.0 all-gather.7.cloned.1.call-start
  282.2 273.4 %all-reduce.5.cloned.1.call-done = f32[1024,1000]{1,0:T(8,128)} async-done(((f32[1024,1000]{1,0:T(8,128)}), f32[1024,1000]{1,0:T(8,128)}) %all-reduce.5.cloned.1.call-update) | async-done | bytes 4096016 | tf_op jit(solution)/shard_map/psum | solution.py:45
  555.6 1.7 fusion.29
  557.3 0.0 all-gather.7.cloned.1.call-update
  557.3 0.2 all-reduce.7.cloned.1.call-start
  557.5 0.0 copy-start.2
  557.6 2.2 multiply_reduce_fusion
  559.8 0.0 copy-done.2
  559.8 3.6 fusion.42
  563.4 56.2 %all-gather.7.cloned.1.call-done = f32[1024,1000]{1,0:T(8,128)} async-done(((f32[64,1000]{1,0:T(8,128)}), f32[1024,1000]{1,0:T(8,128)}) %all-gather.7.cloned.1.call-update) | async-done | bytes 4096016 | tf_op jit(solution)/shard_map/all_gather | solution.py:52
  619.6 0.0 copy-done
  619.6 4.9 fusion.19
  624.6 0.0 copy-start.1
  624.6 0.0 copy-done.4
  624.6 8.6 fusion
  633.2 0.0 all-reduce.7.cloned.1.call-update
  633.2 0.0 all-gather.9.cloned.1.call-start
  633.3 264.6 %all-reduce.7.cloned.1.call-done = f32[1024,1000]{1,0:T(8,128)} async-done(((f32[1024,1000]{1,0:T(8,128)}), f32[1024,1000]{1,0:T(8,128)}) %all-reduce.7.cloned.1.call-update) | async-done | bytes 4096016 | tf_op jit(solution)/shard_map/psum | solution.py:45
  897.9 1.7 fusion.28
  899.6 0.0 all-gather.9.cloned.1.call-update
  899.6 0.0 copy-done.1
  899.6 62.0 %all-gather.9.cloned.1.call-done = f32[1024,1000]{1,0:T(8,128)} async-done(((f32[64,1000]{1,0:T(8,128)}), f32[1024,1000]{1,0:T(8,128)}) %all-gather.9.cloned.1.call-update) | async-done | bytes 4096016 | tf_op jit(solution)/shard_map/all_gather | solution.py:52
  961.7 5.5 fusion.16
  (4 shorter events, 0.1 us)
Async XLA Ops:
  6.5 613.1 %copy-start = (f32[6,64,1024]{2,1,0:T(8,128)S(1)}, f32[6,64,1024]{2,1,0:T(8,128)}, u32[]{:S(2)}) copy-start(f32[6,64,1024]{2,1,0:T(8,128)} %param.8) | copy-start | bytes 4718596
  6.5 1.5 copy-start.5
  6.5 61.9 %all-gather.13.cloned.1.call-start = ((), (), s32[]{:S(2)}) async-start(), calls=%async_computation.5 | async-start | bytes 2228224 | tf_op jit(solution)/shard_map/all_gather | solution.py:29
  11.5 111.2 %all-gather.11.cloned.1.call-start = ((), (), s32[]{:S(2)}) async-start(), calls=%async_computation.4 | async-start | bytes 2228224 | tf_op jit(solution)/shard_map/all_gather | solution.py:29
  12.3 256.6 %all-reduce.9.cloned.1.call-start = ((), (), s32[]{:S(2)}) async-start(), calls=%async_computation.6 | async-start | bytes 8388608 | tf_op jit(solution)/shard_map/psum | solution.py:12
  124.1 431.4 %all-reduce.5.cloned.1.call-start = ((), (), s32[]{:S(2)}) async-start(), calls=%async_computation | async-start | bytes 8388608 | tf_op jit(solution)/shard_map/psum | solution.py:45
  268.9 2.2 copy-start.3
  282.1 337.5 %all-gather.7.cloned.1.call-start = ((), (), s32[]{:S(2)}) async-start(), calls=%async_computation.1 | async-start | bytes 4456448 | tf_op jit(solution)/shard_map/all_gather | solution.py:52
  557.3 340.5 %all-reduce.7.cloned.1.call-start = ((), (), s32[]{:S(2)}) async-start(), calls=%async_computation.2 | async-start | bytes 8388608 | tf_op jit(solution)/shard_map/psum | solution.py:45
  557.5 2.3 copy-start.2
  619.6 5.0 copy-start.4
  624.6 275.0 %copy-start.1 = (f32[6,64,1000]{2,1,0:T(8,128)}, f32[6,64,1000]{2,1,0:T(8,128)S(1)}, u32[]{:S(2)}) copy-start(f32[6,64,1000]{2,1,0:T(8,128)S(1)} %fusion.19) | copy-start | bytes 4608004
  633.2 328.5 %all-gather.9.cloned.1.call-start = ((), (), s32[]{:S(2)}) async-start(), calls=%async_computation.3 | async-start | bytes 4456448 | tf_op jit(solution)/shard_map/all_gather | solution.py:52
Sparse Core Ops, SparseCore 0:
  11.6 56.7 all-gather.12
  71.2 51.4 all-gather.10
  125.4 143.4 all-reduce.8
  282.3 273.2 all-reduce.4
  558.5 61.0 all-gather.6
  633.3 264.4 all-reduce.6
  900.6 61.0 all-gather.8
where the time goes:
time: 974 us
  waiting for transfers between devices  907 us (93%)
  matrix products  33.7 us (3%)
  between operations  17 us (2%)
  other arithmetic  12.2 us (1%)
    psum x2, waiting for transfers between devices, on_device(): summed = lax.psum(products, ('row', 'col'))  538 us
    psum x1, waiting for transfers between devices, broadcast(): return lax.psum(kept, axis)  143 us
    all_gather x2, waiting for transfers between devices, on_device(): full_residual = lax.all_gather(residual, 'col', axis=0, tiled=True)  118 us
    all_gather x2, waiting for transfers between devices, on_device(): full_block = lax.all_gather(own_slice, 'col', axis=0, tiled=True)  107 us
  transfers between devices with their start and end apart: 7, of which 7 were waited for; matrix products, arithmetic and copies ran while one was open for 1% of the time, Pallas kernels for 0%

commit v1 on v0

--- a/solution.py
+++ b/solution.py
@@ -42,7 +42,8 @@
             precision=lax.Precision.HIGHEST,
             preferred_element_type=jnp.float32,
         )
-        summed = lax.psum(products, ("row", "col"))
+        half = lax.psum(products, "row")
+        summed = lax.psum(half, "col")
         own_sum = lax.dynamic_slice_in_dim(summed, my_col * per_col, per_col, 0)
         previous = lax.dynamic_index_in_dim(current, local_index, 0, keepdims=False)
         wanted = lax.dynamic_index_in_dim(targets, local_index, 0, keepdims=False).astype(

time: 974 us -> 1060 us (1.088)
  waiting for transfers between devices: 907 us -> 992 us
    psum x2 -> x4, waiting for transfers between devices: 538 us -> 621 us  [the longest x2 327 us: on_device(): summed = lax.psum(half, 'col')]
  transfers between devices with their start and end apart: 7 -> 9, of which waited for: 7 -> 9; matrix products, arithmetic and copies ran while one was open for 1% -> 1% of each run, Pallas kernels for 0% -> 0%
where the time goes in v1:
time: 1060 us
  waiting for transfers between devices  992 us (94%)
  matrix products  33.7 us (3%)
  between operations  16.7 us (2%)
  other arithmetic  12.2 us (1%)
    psum x2, waiting for transfers between devices, on_device(): summed = lax.psum(half, 'col')  327 us
    psum x2, waiting for transfers between devices, on_device(): half = lax.psum(products, 'row')  293 us
    psum x1, waiting for transfers between devices, broadcast(): return lax.psum(kept, axis)  143 us
    all_gather x2, waiting for transfers between devices, on_device(): full_residual = lax.all_gather(residual, 'col', axis=0, tiled=True)  120 us
    all_gather x2, waiting for transfers between devices, on_device(): full_block = lax.all_gather(own_slice, 'col', axis=0, tiled=True)  107 us
  transfers between devices with their start and end apart: 9, of which 9 were waited for; matrix products, arithmetic and copies ran while one was open for 1% of the time, Pallas kernels for 0%

profile of v1, /device:TPU:1, one launch (start us, length us, event | category | flops | bytes accessed | tf_op | source)
XLA Modules:
  0.0 1058.7 jit_solution(6999389776133725543)
XLA Ops:
  6.5 0.0 copy-start
  6.5 0.0 all-gather.13.cloned.1.call-start
  6.5 1.5 copy.15
  8.1 0.6 fusion.40
  9.8 1.7 constant_dynamic-slice_fusion.2
  11.5 0.0 all-gather.13.cloned.1.call-update
  11.5 0.0 all-gather.11.cloned.1.call-start
  11.6 0.7 all-gather.11.cloned.1.call-update
  12.3 0.0 all-reduce.15.cloned.1.call-start
  14.6 53.9 %all-gather.13.cloned.1.call-done = bf16[1,1024,1024]{2,1,0:T(8,128)(2,1)} async-done(((bf16[1,64,1024]{2,1,0:T(8,128)(2,1)}), bf16[1,1024,1024]{2,1,0:T(8,128)(2,1)}) %all-gather.13.cloned.1.call-update) | async-done | bytes 2097168 | tf_op jit(solution)/shard_map/all_gather | solution.py:29
  68.5 1.5 select_bitcast_fusion
  69.9 52.7 %all-gather.11.cloned.1.call-done = bf16[1,1024,1024]{2,1,0:T(8,128)(2,1)} async-done(((bf16[1,64,1024]{2,1,0:T(8,128)(2,1)}), bf16[1,1024,1024]{2,1,0:T(8,128)(2,1)}) %all-gather.11.cloned.1.call-update) | async-done | bytes 2097168 | tf_op jit(solution)/shard_map/all_gather | solution.py:29
  122.7 1.4 select_bitcast_fusion.1
  124.1 0.0 all-reduce.15.cloned.1.call-update
  124.1 0.0 all-reduce.7.cloned.1.call-start
  124.2 1.4 multiply_reduce_fusion.2
  125.6 0.1 add.79
  125.6 143.2 %all-reduce.15.cloned.1.call-done = (bf16[1024,1024]{1,0:T(8,128)(2,1)}, bf16[1024,1024]{1,0:T(8,128)(2,1)}) async-done(((bf16[1024,1024]{1,0:T(8,128)(2,1)}, bf16[1024,1024]{1,0:T(8,128)(2,1)}), (bf16[1024,1024]{1,0:T(8,128)(2,1)}, bf16[1024,1024]{1,0:T(8,128)(2,1)})) %all-reduce.15.cloned.1.call-update) | async-done | bytes 4194320 | tf_op jit(solution)/shard_map/psum | solution.py:12
  268.9 2.2 multiply_reduce_fusion.1
  271.1 2.4 fusion.41
  273.5 8.6 fusion.7
  282.1 0.0 all-reduce.7.cloned.1.call-update
  282.1 0.0 all-reduce.9.cloned.1.call-start
  282.2 151.3 %all-reduce.7.cloned.1.call-done = f32[1024,1000]{1,0:T(8,128)} async-done(((f32[1024,1000]{1,0:T(8,128)}), f32[1024,1000]{1,0:T(8,128)}) %all-reduce.7.cloned.1.call-update) | async-done | bytes 4096016 | tf_op jit(solution)/shard_map/psum | solution.py:45
  433.5 0.0 all-reduce.9.cloned.1.call-update
  433.5 0.0 all-gather.7.cloned.1.call-start
  433.6 163.6 %all-reduce.9.cloned.1.call-done = f32[1024,1000]{1,0:T(8,128)} async-done(((f32[1024,1000]{1,0:T(8,128)}), f32[1024,1000]{1,0:T(8,128)}) %all-reduce.9.cloned.1.call-update) | async-done | bytes 4096016 | tf_op jit(solution)/shard_map/psum | solution.py:46
  597.2 1.7 fusion.29
  598.9 0.0 all-gather.7.cloned.1.call-update
  599.0 0.2 all-reduce.11.cloned.1.call-start
  599.2 2.2 multiply_reduce_fusion
  601.4 0.0 copy-done.2
  601.5 3.6 fusion.42
  605.0 57.0 %all-gather.7.cloned.1.call-done = f32[1024,1000]{1,0:T(8,128)} async-done(((f32[64,1000]{1,0:T(8,128)}), f32[1024,1000]{1,0:T(8,128)}) %all-gather.7.cloned.1.call-update) | async-done | bytes 4096016 | tf_op jit(solution)/shard_map/all_gather | solution.py:53
  662.1 4.9 fusion.19
  667.0 0.0 copy-start.1
  667.0 0.0 copy-done.4
  667.1 8.6 fusion
  675.7 0.0 all-reduce.11.cloned.1.call-update
  675.7 0.0 all-reduce.13.cloned.1.call-start
  675.7 142.1 %all-reduce.11.cloned.1.call-done = f32[1024,1000]{1,0:T(8,128)} async-done(((f32[1024,1000]{1,0:T(8,128)}), f32[1024,1000]{1,0:T(8,128)}) %all-reduce.11.cloned.1.call-update) | async-done | bytes 4096016 | tf_op jit(solution)/shard_map/psum | solution.py:45
  817.8 0.0 all-reduce.13.cloned.1.call-update
  817.8 0.0 all-gather.9.cloned.1.call-start
  817.9 163.8 %all-reduce.13.cloned.1.call-done = f32[1024,1000]{1,0:T(8,128)} async-done(((f32[1024,1000]{1,0:T(8,128)}), f32[1024,1000]{1,0:T(8,128)}) %all-reduce.13.cloned.1.call-update) | async-done | bytes 4096016 | tf_op jit(solution)/shard_map/psum | solution.py:46
  981.6 1.7 fusion.28
  983.4 0.0 all-gather.9.cloned.1.call-update
  983.5 63.2 %all-gather.9.cloned.1.call-done = f32[1024,1000]{1,0:T(8,128)} async-done(((f32[64,1000]{1,0:T(8,128)}), f32[1024,1000]{1,0:T(8,128)}) %all-gather.9.cloned.1.call-update) | async-done | bytes 4096016 | tf_op jit(solution)/shard_map/all_gather | solution.py:53
  1046.7 5.5 fusion.16
  (10 shorter events, 0.1 us)
Async XLA Ops:
  6.5 655.5 %copy-start = (f32[6,64,1024]{2,1,0:T(8,128)S(1)}, f32[6,64,1024]{2,1,0:T(8,128)}, u32[]{:S(2)}) copy-start(f32[6,64,1024]{2,1,0:T(8,128)} %param.8) | copy-start | bytes 4718596
  6.5 1.5 copy-start.5
  6.5 61.9 %all-gather.13.cloned.1.call-start = ((), (), s32[]{:S(2)}) async-start(), calls=%async_computation.7 | async-start | bytes 2228224 | tf_op jit(solution)/shard_map/all_gather | solution.py:29
  11.5 111.2 %all-gather.11.cloned.1.call-start = ((), (), s32[]{:S(2)}) async-start(), calls=%async_computation.6 | async-start | bytes 2228224 | tf_op jit(solution)/shard_map/all_gather | solution.py:29
  12.3 256.6 %all-reduce.15.cloned.1.call-start = ((), (), s32[]{:S(2)}) async-start(), calls=%async_computation.8 | async-start | bytes 8388608 | tf_op jit(solution)/shard_map/psum | solution.py:12
  124.1 309.3 %all-reduce.7.cloned.1.call-start = ((), (), s32[]{:S(2)}) async-start(), calls=%async_computation | async-start | bytes 8388608 | tf_op jit(solution)/shard_map/psum | solution.py:45
  268.9 2.2 copy-start.3
  282.1 315.1 %all-reduce.9.cloned.1.call-start = ((), (), s32[]{:S(2)}) async-start(), calls=%async_computation.1 | async-start | bytes 8388608 | tf_op jit(solution)/shard_map/psum | solution.py:46
  433.5 228.6 %all-gather.7.cloned.1.call-start = ((), (), s32[]{:S(2)}) async-start(), calls=%async_computation.2 | async-start | bytes 4456448 | tf_op jit(solution)/shard_map/all_gather | solution.py:53
  599.0 218.8 %all-reduce.11.cloned.1.call-start = ((), (), s32[]{:S(2)}) async-start(), calls=%async_computation.3 | async-start | bytes 8388608 | tf_op jit(solution)/shard_map/psum | solution.py:45
  599.2 2.3 copy-start.2
  662.1 5.0 copy-start.4
  667.0 316.4 %copy-start.1 = (f32[6,64,1000]{2,1,0:T(8,128)}, f32[6,64,1000]{2,1,0:T(8,128)S(1)}, u32[]{:S(2)}) copy-start(f32[6,64,1000]{2,1,0:T(8,128)S(1)} %fusion.19) | copy-start | bytes 4608004
  675.7 306.0 %all-reduce.13.cloned.1.call-start = ((), (), s32[]{:S(2)}) async-start(), calls=%async_computation.4 | async-start | bytes 8388608 | tf_op jit(solution)/shard_map/psum | solution.py:46
  817.8 228.9 %all-gather.9.cloned.1.call-start = ((), (), s32[]{:S(2)}) async-start(), calls=%async_computation.5 | async-start | bytes 4456448 | tf_op jit(solution)/shard_map/all_gather | solution.py:53
Sparse Core Ops, SparseCore 0:
  11.6 56.7 all-gather.12
  71.2 51.4 all-gather.10
  125.4 143.4 all-reduce.14
  282.3 151.1 all-reduce.6
  436.0 161.1 all-reduce.8
  599.8 62.2 all-gather.6
  675.8 141.9 all-reduce.10
  820.4 161.1 all-reduce.12
  984.4 62.2 all-gather.8

commit v2 on v0

--- a/solution.py
+++ b/solution.py
@@ -7,9 +7,13 @@
 ridge_weight = 1.0
 
 
+def divide_tables_in(a0, device_axis):
+    return lax.all_gather(a0, axis_name=device_axis).sum(axis=0)
+
+
 def broadcast(value, axis, source):
     kept = jnp.where(lax.axis_index(axis) == source, value, 0).astype(value.dtype)
-    return lax.psum(kept, axis)
+    return divide_tables_in(kept, axis)
 
 
 def on_device(points, targets, coeffs, block_inverse, block_order):

time: 974 us -> 1520 us (1.56)
  waiting for transfers between devices: 907 us -> 1420 us
  other arithmetic: 12.2 us -> 38.4 us
    all_gather x0 -> x2, waiting for transfers between devices: none -> 704 us  [divide_tables_in(): return lax.all_gather(a0, axis_name=device_axis).sum(axis=0)]
    psum x1 -> x0, waiting for transfers between devices: 143 us -> none  [broadcast(): return lax.psum(kept, axis)]
    reduce_sum x0 -> x2, other arithmetic: none -> 26.1 us  [divide_tables_in(): return lax.all_gather(a0, axis_name=device_axis).sum(axis=0)]
    all_gather x2, waiting for transfers between devices: 107 us -> 81.5 us  [on_device(): full_block = lax.all_gather(own_slice, 'col', axis=0, tiled=True)]
  transfers between devices with their start and end apart: 7 -> 8, of which waited for: 7 -> 8; matrix products, arithmetic and copies ran while one was open for 1% -> 3% of each run, Pallas kernels for 0% -> 0%
where the time goes in v2:
time: 1520 us
  waiting for transfers between devices  1420 us (93%)
  other arithmetic  38.4 us (3%)
  matrix products  33.6 us (2%)
  between operations  17.4 us (1%)
    all_gather x2, waiting for transfers between devices, divide_tables_in(): return lax.all_gather(a0, axis_name=device_axis).sum(axis=0)  704 us
    psum x2, waiting for transfers between devices, on_device(): summed = lax.psum(products, ('row', 'col'))  534 us
    all_gather x2, waiting for transfers between devices, on_device(): full_residual = lax.all_gather(residual, 'col', axis=0, tiled=True)  105 us
    all_gather x2, waiting for transfers between devices, on_device(): full_block = lax.all_gather(own_slice, 'col', axis=0, tiled=True)  81.5 us
  transfers between devices with their start and end apart: 8, of which 8 were waited for; matrix products, arithmetic and copies ran while one was open for 3% of the time, Pallas kernels for 0%

profile of v2, /device:TPU:1, one launch (start us, length us, event | category | flops | bytes accessed | tf_op | source)
XLA Modules:
  0.0 1518.6 jit_solution(104090366734618752)
XLA Ops:
  6.5 0.0 copy-start
  6.5 0.0 all-gather.17.cloned.1.call-start
  6.5 1.5 copy.11
  8.1 0.0 copy-done.5
  8.1 0.6 fusion.40
  10.0 1.7 constant_dynamic-slice_fusion.2
  11.6 0.0 all-gather.17.cloned.1.call-update
  11.7 0.0 all-gather.21.cloned.1.call-start
  13.1 55.5 %all-gather.17.cloned.1.call-done = bf16[1,1024,1024]{2,1,0:T(8,128)(2,1)} async-done(((bf16[1,64,1024]{2,1,0:T(8,128)(2,1)}), bf16[1,1024,1024]{2,1,0:T(8,128)(2,1)}) %all-gather.17.cloned.1.call-update) | async-done | bytes 2097168 | tf_op jit(solution)/shard_map/all_gather | solution.py:33
  68.6 1.5 broadcast_select_fusion.1
  70.1 0.0 all-gather.21.cloned.1.call-update
  70.1 0.0 all-gather.19.cloned.1.call-start
  70.2 0.7 all-gather.19.cloned.1.call-update
  70.9 0.0 all-reduce.3.cloned.1.call-start
  70.9 1.4 multiply_reduce_fusion.2
  72.3 0.1 add.71
  72.3 350.3 %all-gather.21.cloned.1.call-done = bf16[1,16384,1024]{2,1,0:T(8,128)(2,1)} async-done(((bf16[1,1024,1024]{2,1,0:T(8,128)(2,1)}), bf16[1,16384,1024]{2,1,0:T(8,128)(2,1)}) %all-gather.21.cloned.1.call-update) | async-done | bytes 33554448 | tf_op jit(solution)/shard_map/all_gather | solution.py:11
  422.6 13.1 reduce_sum.51
  435.7 2.3 multiply_reduce_fusion.1
  438.0 2.4 fusion.41
  440.4 8.6 fusion.7
  449.0 0.0 all-reduce.3.cloned.1.call-update
  449.0 0.0 all-gather.23.cloned.1.call-start
  450.2 26.0 %all-gather.19.cloned.1.call-done = bf16[1,1024,1024]{2,1,0:T(8,128)(2,1)} async-done(((bf16[1,64,1024]{2,1,0:T(8,128)(2,1)}), bf16[1,1024,1024]{2,1,0:T(8,128)(2,1)}) %all-gather.19.cloned.1.call-update) | async-done | bytes 2097168 | tf_op jit(solution)/shard_map/all_gather | solution.py:33
  476.2 1.5 broadcast_select_fusion
  477.6 0.0 all-gather.23.cloned.1.call-update
  477.7 0.0 all-gather.13.cloned.1.call-start
  477.7 269.2 %all-reduce.3.cloned.1.call-done = f32[1024,1000]{1,0:T(8,128)} async-done(((f32[1024,1000]{1,0:T(8,128)}), f32[1024,1000]{1,0:T(8,128)}) %all-reduce.3.cloned.1.call-update) | async-done | bytes 4096016 | tf_op jit(solution)/shard_map/psum | solution.py:49
  746.9 1.7 fusion.29
  748.7 0.0 all-gather.13.cloned.1.call-update
  748.7 0.2 all-reduce.5.cloned.1.call-start
  748.9 353.8 %all-gather.23.cloned.1.call-done = bf16[1,16384,1024]{2,1,0:T(8,128)(2,1)} async-done(((bf16[1,1024,1024]{2,1,0:T(8,128)(2,1)}), bf16[1,16384,1024]{2,1,0:T(8,128)(2,1)}) %all-gather.23.cloned.1.call-update) | async-done | bytes 33554448 | tf_op jit(solution)/shard_map/all_gather | solution.py:11
  1102.8 13.0 reduce_sum.54
  1115.8 2.3 multiply_reduce_fusion
  1118.1 0.1 copy-done.2
  1118.2 3.6 fusion.42
  1121.7 42.5 %all-gather.13.cloned.1.call-done = f32[1024,1000]{1,0:T(8,128)} async-done(((f32[64,1000]{1,0:T(8,128)}), f32[1024,1000]{1,0:T(8,128)}) %all-gather.13.cloned.1.call-update) | async-done | bytes 4096016 | tf_op jit(solution)/shard_map/all_gather | solution.py:56
  1164.3 0.0 copy-done
  1164.3 4.9 fusion.19
  1169.2 0.0 copy-start.1
  1169.3 8.6 fusion
  1177.9 0.0 all-reduce.5.cloned.1.call-update
  1177.9 0.0 all-gather.15.cloned.1.call-start
  1177.9 264.5 %all-reduce.5.cloned.1.call-done = f32[1024,1000]{1,0:T(8,128)} async-done(((f32[1024,1000]{1,0:T(8,128)}), f32[1024,1000]{1,0:T(8,128)}) %all-reduce.5.cloned.1.call-update) | async-done | bytes 4096016 | tf_op jit(solution)/shard_map/psum | solution.py:49
  1442.4 1.7 fusion.28
  1444.1 0.0 all-gather.15.cloned.1.call-update
  1444.2 62.0 %all-gather.15.cloned.1.call-done = f32[1024,1000]{1,0:T(8,128)} async-done(((f32[64,1000]{1,0:T(8,128)}), f32[1024,1000]{1,0:T(8,128)}) %all-gather.15.cloned.1.call-update) | async-done | bytes 4096016 | tf_op jit(solution)/shard_map/all_gather | solution.py:56
  1506.2 5.5 fusion.16
  (9 shorter events, 0.1 us)
Async XLA Ops:
  6.5 1157.7 %copy-start = (f32[6,64,1024]{2,1,0:T(8,128)S(1)}, f32[6,64,1024]{2,1,0:T(8,128)}, u32[]{:S(2)}) copy-start(f32[6,64,1024]{2,1,0:T(8,128)} %param.8) | copy-start | bytes 4718596
  6.5 1.5 copy-start.5
  6.5 62.1 %all-gather.17.cloned.1.call-start = ((), (), s32[]{:S(2)}) async-start(), calls=%async_computation.4 | async-start | bytes 2228224 | tf_op jit(solution)/shard_map/all_gather | solution.py:33
  11.7 411.0 %all-gather.21.cloned.1.call-start = ((), (), s32[]{:S(2)}) async-start(), calls=%async_computation.6 | async-start | bytes 35651584 | tf_op jit(solution)/shard_map/all_gather | solution.py:11
  70.1 406.1 %all-gather.19.cloned.1.call-start = ((), (), s32[]{:S(2)}) async-start(), calls=%async_computation.5 | async-start | bytes 2228224 | tf_op jit(solution)/shard_map/all_gather | solution.py:33
  70.9 676.1 %all-reduce.3.cloned.1.call-start = ((), (), s32[]{:S(2)}) async-start(), calls=%async_computation | async-start | bytes 8388608 | tf_op jit(solution)/shard_map/psum | solution.py:49
  435.7 2.3 copy-start.3
  449.0 653.8 %all-gather.23.cloned.1.call-start = ((), (), s32[]{:S(2)}) async-start(), calls=%async_computation.7 | async-start | bytes 35651584 | tf_op jit(solution)/shard_map/all_gather | solution.py:11
  477.7 686.6 %all-gather.13.cloned.1.call-start = ((), (), s32[]{:S(2)}) async-start(), calls=%async_computation.1 | async-start | bytes 4456448 | tf_op jit(solution)/shard_map/all_gather | solution.py:56
  748.7 693.7 %all-reduce.5.cloned.1.call-start = ((), (), s32[]{:S(2)}) async-start(), calls=%async_computation.2 | async-start | bytes 8388608 | tf_op jit(solution)/shard_map/psum | solution.py:49
  1115.8 2.4 copy-start.2
  1164.3 5.0 copy-start.4
  1169.2 274.9 %copy-start.1 = (f32[6,64,1000]{2,1,0:T(8,128)}, f32[6,64,1000]{2,1,0:T(8,128)S(1)}, u32[]{:S(2)}) copy-start(f32[6,64,1000]{2,1,0:T(8,128)S(1)} %fusion.19) | copy-start | bytes 4608004
  1177.9 328.3 %all-gather.15.cloned.1.call-start = ((), (), s32[]{:S(2)}) async-start(), calls=%async_computation.3 | async-start | bytes 4456448 | tf_op jit(solution)/shard_map/all_gather | solution.py:56
Sparse Core Ops, SparseCore 0:
  11.8 56.7 all-gather.16
  70.4 352.1 all-gather.20
  425.4 50.7 all-gather.18
  481.5 265.3 all-reduce.2
  748.7 354.0 all-gather.22
  1105.8 58.4 all-gather.12
  1178.0 264.3 all-reduce.4
  1445.1 61.0 all-gather.14
